TPU v7x, 32 devices: a whole 2x2x4 slice. The times are simulated.
32 devices in a mesh: groups: 2 (over x), src: 16 (over z, y, core).
Axes of the slice: x: 2, y: 2, z: 4, core: 2. Of those that a mesh axis runs over, the one named last changes fastest.
Arguments:
- layout_mask: int32 [512, 256], P('groups'), parts along dimension 0, may hold values 0 or 1
- source_coords: int32 [32, 2], P('src'), may hold values from -8 to 8
- source_weights: int32 [32], P('src'), may hold values from 1 to 8
- focus_steps: int32 [16], replicated, may hold values from -4 to 4
- pupil_taps: float32 [48], replicated, may hold values from 0.25 to 1.75
- blur_x: float32 [31], replicated, may hold values from 0 to 2
- blur_y: float32 [31], replicated, may hold values from 0 to 2
- blur_z: float32 [31], replicated, may hold values from 0 to 2
Outputs:
- intensity: float32 [8192, 256], P(('groups', 'src')), parts along dimension 0
- latent: float32 [8192, 256], P(('groups', 'src')), parts along dimension 0
There are 2 independent parts, one for each index of `groups`. A program takes and returns all parts, laid end to end along the dimension named above; an argument that names none is the same for every part. Nothing has to cross between parts.
All inputs are finite; a program needn't handle non-finite values.
Results may differ from a plain program's by a relative error of at most 0.0022.
Values sent between devices are 32-bit elements; how exact they have to be, the bound alone decides.
A program may use at most 64 MiB of HBM per device.

v0:
```python
import math

import jax
import jax.numpy as jnp
from jax import lax
from jax.experimental import pallas as pl
from jax.experimental.pallas import tpu as pltpu
from jax.sharding import PartitionSpec as P

two_pi = 2.0 * math.pi
defocus_scale = 0.8
dose_scale = 2.0


def extended_2(block, sides, width):
    for axis, dim in sides:
        count = lax.axis_size(axis)
        forward = [(i, i + 1) for i in range(count - 1)]
        backward = [(target, source) for source, target in forward]
        low = lax.ppermute(
            lax.slice_in_dim(block, block.shape[dim] - width, None, axis=dim), axis, forward
        )
        high = lax.ppermute(lax.slice_in_dim(block, 0, width, axis=dim), axis, backward)
        block = jnp.concatenate([low, block, high], axis=dim)
    return block


def passed_along(block, axis, distance):
    devices = range(lax.axis_size(axis))
    route = [(i - distance, i) for i in devices if i - distance in devices]
    return lax.ppermute(block, axis, route)


def tap_matrix(out_pos, extent, tilt_index, focus_step, pupil_taps):
    tap_count = pupil_taps.shape[0]
    centre = (tap_count - 1) / 2.0
    column_pos = jnp.arange(extent, dtype=jnp.int32)
    offset = column_pos[None, :] - out_pos[:, None] + tap_count // 2
    inside = (offset >= 0) & (offset < tap_count)
    clipped = jnp.clip(offset, 0, tap_count - 1)
    amplitude = jnp.take(pupil_taps, clipped) / math.sqrt(tap_count)
    relative = clipped.astype(jnp.float32) - centre
    phase_angle = (
        two_pi * tilt_index.astype(jnp.float32) * relative / tap_count
        + defocus_scale * focus_step.astype(jnp.float32) * (relative / centre) ** 2
    )
    real_part = jnp.where(inside, amplitude * jnp.cos(phase_angle), jnp.zeros_like(amplitude))
    imag_part = jnp.where(inside, amplitude * jnp.sin(phase_angle), jnp.zeros_like(amplitude))
    return (real_part.astype(jnp.bfloat16), imag_part.astype(jnp.bfloat16))


def field_power(mask_bf, row_pos, tilt_x, tilt_y, focus_step, pupil_taps):
    rows_tile, cols_tile = mask_bf.shape
    row_count = row_pos.shape[0]
    col_pos = jnp.arange(cols_tile, dtype=jnp.int32)
    rows_real, rows_imag = tap_matrix(row_pos, rows_tile, tilt_y, focus_step, pupil_taps)
    cols_real, cols_imag = tap_matrix(col_pos, cols_tile, tilt_x, focus_step, pupil_taps)
    stacked = jnp.concatenate([rows_real, rows_imag], axis=0)
    first_pass = jnp.dot(stacked, mask_bf, preferred_element_type=jnp.float32).astype(jnp.bfloat16)
    joined = jnp.concatenate([first_pass[:row_count], first_pass[row_count:]], axis=1)
    upper_half = jnp.concatenate([cols_real.T, cols_imag.T], axis=1)
    lower_half = jnp.concatenate([-cols_imag.T, cols_real.T], axis=1)
    pupil_cols = jnp.concatenate([upper_half, lower_half], axis=0)
    field_parts = jnp.dot(joined, pupil_cols, preferred_element_type=jnp.float32)
    return field_parts[:, :cols_tile] ** 2 + field_parts[:, cols_tile:] ** 2


def on_device(
    layout_mask, source_coords, source_weights, focus_steps, pupil_taps, blur_x, blur_y, blur_z
):
    rows_tile, cols_tile = layout_mask.shape
    planes = focus_steps.shape[0]
    devices = lax.axis_size("src")
    src_local = source_coords.shape[0]
    mask_bf = layout_mask.astype(jnp.bfloat16)
    own_rows = planes * rows_tile // devices
    per_plane = devices // planes
    factors = source_weights.astype(jnp.float32) / (4.0 * src_local * devices)
    row_pos = jnp.arange(rows_tile, dtype=jnp.int32)

    def plane_term(focus_step):
        running = jnp.zeros((rows_tile, cols_tile), jnp.float32)
        for source in range(src_local):
            power = field_power(
                mask_bf,
                row_pos,
                source_coords[source, 0],
                source_coords[source, 1],
                focus_step,
                pupil_taps,
            )
            running = running + factors[source] * power
        return running

    partial_sum = lax.map(plane_term, focus_steps).reshape(planes * rows_tile, cols_tile)
    intensity = lax.psum_scatter(partial_sum, "src", scatter_dimension=0, tiled=True)
    acid_level = 1.0 - jnp.exp(-dose_scale * intensity)
    width_x = blur_x.shape[0]
    half_x = width_x // 2
    padded = jnp.pad(acid_level, ((0, 0), (half_x, half_x)))
    along_x = jnp.zeros_like(acid_level)
    for tap_index in range(width_x):
        along_x = (
            along_x + blur_x[tap_index] / width_x * padded[:, tap_index : tap_index + cols_tile]
        )
    width_y = blur_y.shape[0]
    half_y = width_y // 2
    extended = extended_2(along_x, (("src", 0),), half_y)
    along_y = jnp.zeros_like(along_x)
    for tap_index in range(width_y):
        along_y = along_y + blur_y[tap_index] / width_y * extended[tap_index : tap_index + own_rows]
    latent = blur_z[planes - 1] / planes * along_y
    for plane_lag in range(1 - planes, planes):
        if plane_lag != 0:
            arrived = passed_along(along_y, "src", plane_lag * per_plane)
            latent = latent + blur_z[plane_lag + planes - 1] / planes * arrived
    return (intensity, latent)


max_shift = 8
shifts = 2 * max_shift + 1
lanes = 512


def exact_dot(left, right):
    def halves(value):
        high = value.astype(jnp.bfloat16)
        return high, (value - high.astype(jnp.float32)).astype(jnp.bfloat16)

    def product(a, b):
        return jnp.dot(a, b, preferred_element_type=jnp.float32)

    left_high, left_low = halves(left)
    right_high, right_low = halves(right)
    return (
        product(left_high, right_low) + product(left_low, right_high)
    ) + product(left_high, right_high)


def store_toeplitz(row, position, pieces, apart=128):
    base = pltpu.roll(jnp.broadcast_to(row, (16, 128)), 0, 1, stride=1, stride_axis=0)
    lane = lax.broadcasted_iota(jnp.int32, (16, 128), 1)
    zero = jnp.zeros((16, 128), jnp.float32)
    for j in range(8):
        first = 16 * j + position - 256
        turn, tile = first % 128, first // 128
        rolled = pltpu.roll(base, turn, 1) if turn else base
        wraps = turn > 65
        kept = jnp.where(lane >= turn, rolled, zero) if wraps else rolled
        wrapped = jnp.where(lane < turn, rolled, zero) if wraps else zero
        for block, start in ((j, tile), (j + 8, tile + 1)):
            for column in range(2):
                part = kept if column == start else wrapped if column == start + 1 else zero
                for ref, top, side, sign in pieces:
                    value = part if sign > 0 else -part
                    left = side + apart * column
                    ref[top + 16 * block : top + 16 * block + 16, left : left + 128] = (
                        value.astype(ref.dtype)
                    )


def store_taps(taps_ref, row, focus, flip, real_ref, imag_ref, tap_count):
    centre = (tap_count - 1) / 2.0
    amplitude = taps_ref[row : row + 1, :128] / math.sqrt(tap_count)
    shape = (24, 128)
    relative = (lax.broadcasted_iota(jnp.int32, shape, 1).astype(jnp.float32) - centre) * flip
    tilt = (lax.broadcasted_iota(jnp.int32, shape, 0) - max_shift).astype(jnp.float32)
    phase = (
        two_pi * tilt * relative / tap_count + defocus_scale * focus * (relative / centre) ** 2
    )
    real_ref[...] = amplitude * jnp.cos(phase)
    imag_ref[...] = amplitude * jnp.sin(phase)


def build_tables(tap_count, mask_ref, rows_ref, focus, tap_refs, stacked_slots, fields, pupils):
    forward_real, forward_imag, back_real, back_imag = tap_refs
    store_taps(rows_ref, 0, focus, 1.0, forward_real, forward_imag, tap_count)
    store_taps(rows_ref, 1, focus, -1.0, back_real, back_imag, tap_count)
    mask_bf = mask_ref[...].astype(jnp.float32).astype(jnp.bfloat16)

    def one_shift(shift, slot):
        stacked = stacked_slots.at[slot]
        row = pl.ds(shift, 1)
        store_toeplitz(forward_real[row, :], 232, ((stacked, 0, 0, 1),))
        store_toeplitz(forward_imag[row, :], 232, ((stacked, 256, 0, 1),))
        first = jnp.dot(stacked[...], mask_bf, preferred_element_type=jnp.float32)
        fields[shift, :, :256] = first[:256].astype(jnp.bfloat16)
        fields[shift, :, 256:] = first[256:].astype(jnp.bfloat16)
        pupil = pupils.at[shift]
        store_toeplitz(back_real[row, :], 233, ((pupil, 0, 0, 1), (pupil, 256, 128, 1)), 256)
        store_toeplitz(back_imag[row, :], 233, ((pupil, 0, 128, 1), (pupil, 256, 0, -1)), 256)

    def four_shifts(step, carry):
        for slot in range(4):
            one_shift(4 * step + slot, slot)
        return carry

    lax.fori_loop(0, shifts // 4, four_shifts, 0)
    one_shift(shifts - 1, 0)


def lane_row(count, value):
    lane = lax.broadcasted_iota(jnp.int32, (1, lanes), 1)
    row = jnp.zeros((1, lanes), jnp.float32)
    for t in range(count):
        row = jnp.where(lane == t, value(t), row)
    return row


def plane_kernel(
    n, wide, mask_hbm, coords_hbm, weights_hbm, focus_hbm, taps_hbm, blur_x_hbm, blur_y_hbm,
    blur_z_hbm, intensity_ref, latent_ref, mask_ref, coords_ref, weights_ref, focus_ref, taps_ref,
    blur_x_ref, blur_y_ref, blur_z_ref, arg_sems, rows, t0, t1, t2, t3, stacked, fields, pupils, blur,
    centre, mix, own, points, points_smem, along, columns, mixed, planes, send_sems, recv_sems,
    local_sem,
):
    me = lax.axis_index("src")
    group = lax.axis_index("groups")
    local = weights_ref.shape[0]
    tap_count, blur_count = taps_ref.shape[0], blur_x_ref.shape[0]
    barrier = pltpu.get_barrier_semaphore()

    def each(action):
        lax.fori_loop(1, n, lambda off, carry: (action(off), carry)[1], 0)

    def peer(off):
        return (group, lax.rem(me + off, n))

    def signal(off):
        pl.semaphore_signal(
            barrier, inc=1, device_id=peer(off), device_id_type=pl.DeviceIdType.MESH
        )

    def copy(phase, source, target, off, slot):
        return pltpu.make_async_remote_copy(
            src_ref=source(off),
            dst_ref=target.at[slot],
            send_sem=send_sems.at[phase, off],
            recv_sem=recv_sems.at[phase, off],
            device_id=peer(off),
            device_id_type=pl.DeviceIdType.MESH,
        )

    def block_of(device):
        return device // 2 + lax.rem(device, 2) * (n // 2)

    def itself(device):
        return device

    def start(phase, source, target, place=itself, wanted=None):
        def one(off):
            transfer = copy(phase, source, target, off, place(me))
            if wanted is None:
                transfer.start()
            else:
                pl.when(wanted(block_of(lax.rem(me + off, n))))(transfer.start)

        each(one)

    def receive(phase, source, target, place=itself):
        each(
            lambda off: copy(
                phase, source, target, off, place(lax.rem(me + n - off, n))
            ).wait_recv()
        )

    def sent(phase, source, target, place=itself):
        each(lambda off: copy(phase, source, target, off, place(me)).wait_send())

    fetches = [
        pltpu.make_async_copy(source, target, arg_sems.at[place])
        for place, (source, target) in enumerate(
            (
                (coords_hbm, coords_ref),
                (weights_hbm, weights_ref),
                (focus_hbm, focus_ref),
                (taps_hbm, taps_ref),
                (blur_x_hbm, blur_x_ref),
                (blur_y_hbm, blur_y_ref),
                (blur_z_hbm, blur_z_ref),
                (mask_hbm, mask_ref),
            )
        )
    ]
    for fetch in fetches:
        fetch.start()
    each(signal)
    for fetch in fetches:
        fetch.wait()
    lane = lax.broadcasted_iota(jnp.int32, (1, 128), 1)
    packed = jnp.zeros((1, 128), jnp.int32)
    for s in range(local):
        packed = jnp.where(lane == 3 * s, coords_ref[s, 0], packed)
        packed = jnp.where(lane == 3 * s + 1, coords_ref[s, 1], packed)
        packed = jnp.where(lane == 3 * s + 2, weights_ref[s], packed)
    own[...] = packed
    points[me] = packed
    rows[0:1, :] = lane_row(tap_count, lambda t: taps_ref[t])
    rows[1:2, :] = lane_row(tap_count, lambda t: taps_ref[tap_count - 1 - t])
    rows[2:3, :] = lane_row(blur_count, lambda t: blur_x_ref[t] / blur_count)
    rows[3:4, :] = lane_row(blur_count, lambda t: blur_y_ref[blur_count - 1 - t] / blur_count)
    pl.semaphore_wait(barrier, n - 1)
    point_source = lambda off: own
    start(0, point_source, points)

    focus = focus_ref[me].astype(jnp.float32)
    build_tables(tap_count, mask_ref, rows, focus, (t0, t1, t2, t3), stacked, fields, pupils)
    store_toeplitz(rows[2:3, :128], 241, ((blur, 0, 0, 1),))
    intensity_ref[...] = jnp.zeros_like(intensity_ref)
    receive(0, point_source, points)
    to_smem = pltpu.make_async_copy(points, points_smem, local_sem)
    to_smem.start()
    to_smem.wait()

    def image_half(half):
        def four_devices(step, carry):
            power = jnp.zeros((256, 128), jnp.float32)
            for place in range(4 * local):
                device, s = 4 * step + place // local, place % local
                point = [points_smem[device, 0, 3 * s + item] for item in range(3)]
                factor = point[2].astype(jnp.float32) / (4.0 * local * n)
                field = jnp.dot(
                    fields[point[1] + max_shift],
                    pupils[point[0] + max_shift, :, 256 * half : 256 * half + 256],
                    preferred_element_type=jnp.float32,
                )
                power = power + factor * (field[:, :128] ** 2 + field[:, 128:] ** 2)
            intensity_ref[:, 128 * half : 128 * half + 128] += power
            return carry

        lax.fori_loop(0, n // 4, four_devices, 0)

    def acid_columns(stop):
        return (1.0 - jnp.exp(-dose_scale * intensity_ref[:, :stop])).T

    early = (128 - blur_count // 2) // wide
    column_source = lambda off: along.at[block_of(lax.rem(me + off, n))]
    image_half(0)
    along[:early] = exact_dot(blur[: early * wide, :128], acid_columns(128)).reshape(
        early, wide, 256
    )
    start(1, column_source, columns, wanted=lambda block: block < early)
    image_half(1)
    along[early:] = exact_dot(blur[early * wide :, :], acid_columns(256)).reshape(
        n - early, wide, 256
    )
    start(1, column_source, columns, wanted=lambda block: block >= early)
    columns[me] = along[block_of(me)]

    back_y = rows[3:4, :]
    store_toeplitz(rows[3:4, :128], 241, ((centre, 0, 0, 1),))
    tall = jnp.broadcast_to(back_y, (16, lanes))
    before = pltpu.roll(tall, lanes - 31, 1, stride=1, stride_axis=0)[:, :256]
    after = pltpu.roll(tall, 241, 1, stride=1, stride_axis=0)[:, :256]
    pad = jnp.zeros((112, 256), jnp.float32)
    distance = lax.broadcasted_iota(jnp.int32, (256, 256), 0) - lax.broadcasted_iota(
        jnp.int32, (256, 256), 1
    )
    mix[...] = jnp.zeros_like(mix)
    for lag in range(1 - n, n):
        mix[...] = jnp.where(distance == lag * wide, blur_z_ref[lag + n - 1] / n, mix[...])

    receive(1, column_source, columns)
    stack = columns[...].reshape(256, 256)
    zero = jnp.zeros((wide, 128), jnp.float32)
    along_y = (
        exact_dot(stack, centre[...])
        + exact_dot(
            jnp.concatenate([zero, stack[:-wide, 128:]], axis=0),
            jnp.concatenate([pad, before], axis=0),
        )
        + exact_dot(
            jnp.concatenate([stack[wide:, :128], zero], axis=0),
            jnp.concatenate([after, pad], axis=0),
        )
    )
    mixed[...] = exact_dot(mix[...], along_y).reshape(n, wide, 256)
    plane_source = lambda off: mixed.at[lax.rem(me + off, n)]
    start(2, plane_source, planes, block_of)
    planes[block_of(me)] = mixed[me]
    sent(0, point_source, points)
    sent(1, column_source, columns)
    receive(2, plane_source, planes, block_of)
    latent_ref[...] = planes[...].reshape(256, 256).T
    sent(2, plane_source, planes, block_of)


def plane_per_device(
    layout_mask, source_coords, source_weights, focus_steps, pupil_taps, blur_x, blur_y, blur_z
):
    n = lax.axis_size("src")
    wide = layout_mask.shape[1] // n
    square = jax.ShapeDtypeStruct((256, 256), jnp.float32)
    full = pltpu.VMEM((256, 256), jnp.float32)
    parts = pltpu.VMEM((n, wide, 256), jnp.float32)
    vmem = pl.BlockSpec(memory_space=pltpu.VMEM)
    hbm = pl.BlockSpec(memory_space=pltpu.HBM)
    arguments = (
        source_coords, source_weights, focus_steps, pupil_taps, blur_x, blur_y, blur_z
    )
    return pl.pallas_call(
        lambda *refs: plane_kernel(n, wide, *refs),
        out_shape=(square, square),
        in_specs=[hbm] * 8,
        out_specs=(vmem, vmem),
        scratch_shapes=[pltpu.VMEM((256, 256), jnp.int32)]
        + [pltpu.SMEM(value.shape, value.dtype) for value in arguments]
        + [pltpu.SemaphoreType.DMA((8,)), pltpu.VMEM((8, lanes), jnp.float32)]
        + [pltpu.VMEM((24, 128), jnp.float32)] * 4
        + [
            pltpu.VMEM((4, 512, 256), jnp.bfloat16),
            pltpu.VMEM((shifts, 256, 512), jnp.bfloat16),
            pltpu.VMEM((shifts, 512, 512), jnp.bfloat16),
            full,
            full,
            full,
            pltpu.VMEM((1, 128), jnp.int32),
            pltpu.VMEM((n, 1, 128), jnp.int32),
            pltpu.SMEM((n, 1, 128), jnp.int32),
            parts,
            parts,
            parts,
            parts,
            pltpu.SemaphoreType.DMA((3, n)),
            pltpu.SemaphoreType.DMA((3, n)),
            pltpu.SemaphoreType.DMA,
        ],
        compiler_params=pltpu.CompilerParams(
            vmem_limit_bytes=64 * 2**20 - 2**17, collective_id=0, has_side_effects=True
        ),
    )(layout_mask, *arguments)


def solution(mesh):
    in_specs = (P("groups", None), P("src", None), P("src"), P(), P(), P(), P(), P())
    out_specs = (P(("groups", "src"), None), P(("groups", "src"), None))
    body = plane_per_device if mesh.shape["src"] == 16 else on_device
    return jax.shard_map(
        body, mesh=mesh, in_specs=in_specs, out_specs=out_specs, check_vma=False
    )
```

profile of v0, /device:TPU:0, one launch (start us, length us, event | category | flops | bytes accessed | tf_op | source)
XLA Modules:
  0.0 34.4 jit_solution(4760234390805929670)
XLA Ops:
  0.6 31.3 %shard_map.95 = (f32[256,256]{1,0:T(8,128)}, f32[256,256]{1,0:T(8,128)}) custom-call(s32[256,256]{1,0:T(8,128)} %refs_0_.1, s32[2,2]{1,0:T(2,128)} %refs_1_.1, s32[2]{0:T(128)} %refs_2_.1, s32[16]{0:T(128)} %refs_3_.1, f32[48]{0:T(128)} %refs_4_.1, f32[31]{0:T(128)} %refs_5_.1, f32[31]{0:T(128)} %refs_6_.1, f32[31]{0:T(128)} %refs_7_.1), custom_call_target="tpu_custom_call" | custom-call | tf_op jit(solution)/shard_map/pallas_call | solution.py:401
  32.0 0.0 copy-start
  32.0 1.7 %copy.12 = f32[256,256]{1,0:T(8,128)} copy(f32[256,256]{1,0:T(8,128)} %get-tuple-element.4) | data formatting | bytes 524288
  33.7 0.0 copy-done
  33.7 0.7 %copy.13 = f32[256,256]{1,0:T(8,128)} copy(f32[256,256]{1,0:T(8,128)S(1)} %copy-done) | data formatting | bytes 524288
Async XLA Ops:
  32.0 1.7 %copy-start = (f32[256,256]{1,0:T(8,128)S(1)}, f32[256,256]{1,0:T(8,128)}, u32[]{:S(2)}) copy-start(f32[256,256]{1,0:T(8,128)} %get-tuple-element.5) | copy-start | bytes 786436
where the time goes:
time: 34.5 us; the launch traced here: 34.4 us
  Pallas kernels  31.3 us (91%)
  local copies, waits for them, and re-layouts  2.42 us (7%)
  between operations  0.65 us (2%)
    pallas_call x1, Pallas kernels, plane_per_device(): pl.pallas_call(lambda *refs: plane_kernel(n, wide, *refs), out_shape=(squ...  31.3 us
    unnamed x4, local copies, waits for them, and re-layouts  2.42 us

commit v1 on v0

--- a/solution.py
+++ b/solution.py
@@ -120,6 +120,7 @@
 max_shift = 8
 shifts = 2 * max_shift + 1
 lanes = 512
+devices_unrolled = 16
 
 
 def exact_dot(left, right):
@@ -172,23 +173,62 @@
     imag_ref[...] = amplitude * jnp.sin(phase)
 
 
-def build_tables(tap_count, mask_ref, rows_ref, focus, tap_refs, stacked_slots, fields, pupils):
-    forward_real, forward_imag, back_real, back_imag = tap_refs
-    store_taps(rows_ref, 0, focus, 1.0, forward_real, forward_imag, tap_count)
-    store_taps(rows_ref, 1, focus, -1.0, back_real, back_imag, tap_count)
-    mask_bf = mask_ref[...].astype(jnp.float32).astype(jnp.bfloat16)
+def toeplitz_tiles(row, position, blocks):
+    base = pltpu.roll(jnp.broadcast_to(row, (16, 128)), 0, 1, stride=1, stride_axis=0)
+    apart = lax.broadcasted_iota(jnp.int32, (16, 128), 1) - lax.broadcasted_iota(
+        jnp.int32, (16, 128), 0
+    )
+    tiles = {}
+    for block in blocks:
+        turn = 16 * block - position
+        tile = pltpu.roll(base, turn % 128, 1) if turn % 128 else base
+        if 127 - turn >= 128:
+            tile = jnp.where(apart < 128 + turn, tile, 0.0)
+        if -15 - turn < -80:
+            tile = jnp.where(apart >= turn - 80, tile, 0.0)
+        tiles[block] = tile
+    return tiles
+
+
+def build_columns(forward_real, forward_imag, shapes):
+    def one_shift(shift):
+        row = pl.ds(shift, 1)
+        real = toeplitz_tiles(forward_real[row, :], 24, range(8))
+        imag = toeplitz_tiles(forward_imag[row, :], 24, range(8))
+        for j in range(8):
+            re, im = real[j].astype(jnp.bfloat16), imag[j].astype(jnp.bfloat16)
+            upper, lower = slice(16 * j, 16 * j + 16), slice(128 + 16 * j, 144 + 16 * j)
+            shapes[shift, upper, :128] = re
+            shapes[shift, upper, 128:] = -im
+            shapes[shift, lower, :128] = im
+            shapes[shift, lower, 128:] = re
+
+    def four_shifts(step, carry):
+        for place in range(4):
+            one_shift(4 * step + place)
+        return carry
+
+    lax.fori_loop(0, shifts // 4, four_shifts, 0)
+    one_shift(shifts - 1)
+
+
+def build_fields(back_real, back_imag, mask_ref, slots, fields):
+    mask_turned = mask_ref[...].astype(jnp.float32).T.astype(jnp.bfloat16)
 
     def one_shift(shift, slot):
-        stacked = stacked_slots.at[slot]
         row = pl.ds(shift, 1)
-        store_toeplitz(forward_real[row, :], 232, ((stacked, 0, 0, 1),))
-        store_toeplitz(forward_imag[row, :], 232, ((stacked, 256, 0, 1),))
-        first = jnp.dot(stacked[...], mask_bf, preferred_element_type=jnp.float32)
-        fields[shift, :, :256] = first[:256].astype(jnp.bfloat16)
-        fields[shift, :, 256:] = first[256:].astype(jnp.bfloat16)
-        pupil = pupils.at[shift]
-        store_toeplitz(back_real[row, :], 233, ((pupil, 0, 0, 1), (pupil, 256, 128, 1)), 256)
-        store_toeplitz(back_imag[row, :], 233, ((pupil, 0, 128, 1), (pupil, 256, 0, -1)), 256)
+        for side, source in ((0, back_real), (256, back_imag)):
+            tiles = toeplitz_tiles(source[row, :], 23, range(-2, 10))
+            for block, tile in tiles.items():
+                value = tile.astype(jnp.bfloat16)
+                if block >= 0:
+                    slots[slot, 16 * block : 16 * block + 16, side : side + 128] = value
+                if block < 8:
+                    top = 16 * block + 128
+                    slots[slot, top : top + 16, side + 128 : side + 256] = value
+        fields[shift] = jnp.dot(
+            mask_turned, slots[slot], preferred_element_type=jnp.float32
+        ).astype(jnp.bfloat16)
 
     def four_shifts(step, carry):
         for slot in range(4):
@@ -210,8 +250,8 @@
 def plane_kernel(
     n, wide, mask_hbm, coords_hbm, weights_hbm, focus_hbm, taps_hbm, blur_x_hbm, blur_y_hbm,
     blur_z_hbm, intensity_ref, latent_ref, mask_ref, coords_ref, weights_ref, focus_ref, taps_ref,
-    blur_x_ref, blur_y_ref, blur_z_ref, arg_sems, rows, t0, t1, t2, t3, stacked, fields, pupils, blur,
-    centre, mix, own, points, points_smem, along, columns, mixed, planes, send_sems, recv_sems,
+    blur_x_ref, blur_y_ref, blur_z_ref, arg_sems, rows, t0, t1, t2, t3, slots, fields, shapes, image,
+    acid, centre, mix, own, points, points_smem, along, columns, mixed, planes, send_sems, recv_sems,
     local_sem,
 ):
     me = lax.axis_index("src")
@@ -241,31 +281,19 @@
             device_id_type=pl.DeviceIdType.MESH,
         )
 
-    def block_of(device):
-        return device // 2 + lax.rem(device, 2) * (n // 2)
-
-    def itself(device):
-        return device
-
-    def start(phase, source, target, place=itself, wanted=None):
-        def one(off):
-            transfer = copy(phase, source, target, off, place(me))
-            if wanted is None:
-                transfer.start()
-            else:
-                pl.when(wanted(block_of(lax.rem(me + off, n))))(transfer.start)
-
-        each(one)
-
-    def receive(phase, source, target, place=itself):
+    def start(phase, source, target):
+        each(lambda off: copy(phase, source, target, off, me).start())
+
+    def receive(phase, source, target):
         each(
-            lambda off: copy(
-                phase, source, target, off, place(lax.rem(me + n - off, n))
-            ).wait_recv()
-        )
-
-    def sent(phase, source, target, place=itself):
-        each(lambda off: copy(phase, source, target, off, place(me)).wait_send())
+            lambda off: copy(phase, source, target, off, lax.rem(me + n - off, n)).wait_recv()
+        )
+
+    def sent(phase, source, target):
+        each(lambda off: copy(phase, source, target, off, me).wait_send())
+
+    def blocks(ref, part):
+        return lambda off: ref.at[part, lax.rem(me + off, n)]
 
     fetches = [
         pltpu.make_async_copy(source, target, arg_sems.at[place])
@@ -285,6 +313,7 @@
     for fetch in fetches:
         fetch.start()
     each(signal)
+    slots[...] = jnp.zeros_like(slots)
     for fetch in fetches:
         fetch.wait()
     lane = lax.broadcasted_iota(jnp.int32, (1, 128), 1)
@@ -299,100 +328,132 @@
     rows[1:2, :] = lane_row(tap_count, lambda t: taps_ref[tap_count - 1 - t])
     rows[2:3, :] = lane_row(blur_count, lambda t: blur_x_ref[t] / blur_count)
     rows[3:4, :] = lane_row(blur_count, lambda t: blur_y_ref[blur_count - 1 - t] / blur_count)
+    focus = focus_ref[me].astype(jnp.float32)
+    store_taps(rows, 0, focus, 1.0, t0, t1, tap_count)
+    store_taps(rows, 1, focus, -1.0, t2, t3, tap_count)
+    build_columns(t0, t1, shapes)
     pl.semaphore_wait(barrier, n - 1)
     point_source = lambda off: own
     start(0, point_source, points)
-
-    focus = focus_ref[me].astype(jnp.float32)
-    build_tables(tap_count, mask_ref, rows, focus, (t0, t1, t2, t3), stacked, fields, pupils)
-    store_toeplitz(rows[2:3, :128], 241, ((blur, 0, 0, 1),))
-    intensity_ref[...] = jnp.zeros_like(intensity_ref)
-    receive(0, point_source, points)
-    to_smem = pltpu.make_async_copy(points, points_smem, local_sem)
-    to_smem.start()
-    to_smem.wait()
-
-    def image_half(half):
-        def four_devices(step, carry):
-            power = jnp.zeros((256, 128), jnp.float32)
-            for place in range(4 * local):
-                device, s = 4 * step + place // local, place % local
-                point = [points_smem[device, 0, 3 * s + item] for item in range(3)]
-                factor = point[2].astype(jnp.float32) / (4.0 * local * n)
-                field = jnp.dot(
-                    fields[point[1] + max_shift],
-                    pupils[point[0] + max_shift, :, 256 * half : 256 * half + 256],
-                    preferred_element_type=jnp.float32,
-                )
-                power = power + factor * (field[:, :128] ** 2 + field[:, 128:] ** 2)
-            intensity_ref[:, 128 * half : 128 * half + 128] += power
-            return carry
-
-        lax.fori_loop(0, n // 4, four_devices, 0)
-
-    def acid_columns(stop):
-        return (1.0 - jnp.exp(-dose_scale * intensity_ref[:, :stop])).T
-
-    early = (128 - blur_count // 2) // wide
-    column_source = lambda off: along.at[block_of(lax.rem(me + off, n))]
-    image_half(0)
-    along[:early] = exact_dot(blur[: early * wide, :128], acid_columns(128)).reshape(
-        early, wide, 256
-    )
-    start(1, column_source, columns, wanted=lambda block: block < early)
-    image_half(1)
-    along[early:] = exact_dot(blur[early * wide :, :], acid_columns(256)).reshape(
-        n - early, wide, 256
-    )
-    start(1, column_source, columns, wanted=lambda block: block >= early)
-    columns[me] = along[block_of(me)]
-
+    build_fields(t2, t3, mask_ref, slots, fields)
+    image[...] = jnp.zeros_like(image)
+    tiles = toeplitz_tiles(rows[2:3, :128], 15, range(-1, 9))
+    blank = jnp.zeros((96, 128), jnp.float32)
+    blur_first = jnp.concatenate([tiles[j] for j in range(4)], axis=0)[:, :96]
+    blur_last = jnp.concatenate([tiles[j] for j in range(2, 6)], axis=0)[:, :96]
+    blur_middle = jnp.concatenate(
+        [
+            jnp.concatenate([tiles[j] for j in range(1, 9)], axis=0),
+            jnp.concatenate([blank, tiles[-1], tiles[0]], axis=0)[:, :32],
+        ],
+        axis=1,
+    )
     back_y = rows[3:4, :]
     store_toeplitz(rows[3:4, :128], 241, ((centre, 0, 0, 1),))
     tall = jnp.broadcast_to(back_y, (16, lanes))
     before = pltpu.roll(tall, lanes - 31, 1, stride=1, stride_axis=0)[:, :256]
     after = pltpu.roll(tall, 241, 1, stride=1, stride_axis=0)[:, :256]
     pad = jnp.zeros((112, 256), jnp.float32)
-    distance = lax.broadcasted_iota(jnp.int32, (256, 256), 0) - lax.broadcasted_iota(
-        jnp.int32, (256, 256), 1
-    )
-    mix[...] = jnp.zeros_like(mix)
+    size = n * wide
+    distance = lax.broadcasted_iota(jnp.int32, (size, size), 0) - lax.broadcasted_iota(
+        jnp.int32, (size, size), 1
+    )
+    mixing = jnp.zeros((size, size), jnp.float32)
     for lag in range(1 - n, n):
-        mix[...] = jnp.where(distance == lag * wide, blur_z_ref[lag + n - 1] / n, mix[...])
-
-    receive(1, column_source, columns)
-    stack = columns[...].reshape(256, 256)
-    zero = jnp.zeros((wide, 128), jnp.float32)
-    along_y = (
-        exact_dot(stack, centre[...])
-        + exact_dot(
-            jnp.concatenate([zero, stack[:-wide, 128:]], axis=0),
-            jnp.concatenate([pad, before], axis=0),
-        )
-        + exact_dot(
-            jnp.concatenate([stack[wide:, :128], zero], axis=0),
-            jnp.concatenate([after, pad], axis=0),
-        )
-    )
-    mixed[...] = exact_dot(mix[...], along_y).reshape(n, wide, 256)
-    plane_source = lambda off: mixed.at[lax.rem(me + off, n)]
-    start(2, plane_source, planes, block_of)
-    planes[block_of(me)] = mixed[me]
+        mixing = jnp.where(distance == lag * wide, blur_z_ref[lag + n - 1] / n, mixing)
+    mix[...] = mixing
+    receive(0, point_source, points)
+    to_smem = pltpu.make_async_copy(points, points_smem, local_sem)
+    to_smem.start()
+    to_smem.wait()
+
+    def image_columns(left, low, high, first):
+        count = high - low
+
+        def some_devices(step, carry):
+            power = jnp.zeros((count, 256), jnp.float32)
+            for place in range(devices_unrolled * local):
+                device, s = devices_unrolled * step + place // local, place % local
+                point = [points_smem[device, 0, 3 * s + item] for item in range(3)]
+                factor = point[2].astype(jnp.float32) / (4.0 * local * n)
+                column, row = point[0] + max_shift, point[1] + max_shift
+                field = jnp.dot(
+                    jnp.concatenate(
+                        [shapes[column, low:high], shapes[column, 128 + low : 128 + high]], axis=0
+                    ),
+                    jnp.concatenate(
+                        [
+                            fields[row, first : first + 128, :256],
+                            fields[row, first : first + 128, 256:],
+                        ],
+                        axis=0,
+                    ),
+                    preferred_element_type=jnp.float32,
+                )
+                power = power + factor * (field[:count] ** 2 + field[count:] ** 2)
+            image[left : left + count] += power
+            return carry
+
+        lax.fori_loop(0, n // devices_unrolled, some_devices, 0)
+        acid[left : left + count] = 1.0 - jnp.exp(-dose_scale * image[left : left + count])
+
+    def send_columns(part, values):
+        along[part] = values.reshape(n, wide, 256)
+        start(1 + part, blocks(along, part), columns.at[part])
+        columns[part, me] = along[part, me]
+
+    def mix_planes(part):
+        receive(1 + part, blocks(along, part), columns.at[part])
+        stack = columns[part].reshape(size, 256)
+        zero = jnp.zeros((wide, 128), jnp.float32)
+        along_y = (
+            exact_dot(stack, centre[...])
+            + exact_dot(
+                jnp.concatenate([zero, stack[:-wide, 128:]], axis=0),
+                jnp.concatenate([pad, before], axis=0),
+            )
+            + exact_dot(
+                jnp.concatenate([stack[wide:, :128], zero], axis=0),
+                jnp.concatenate([after, pad], axis=0),
+            )
+        )
+        mixed[part] = exact_dot(mix[...], along_y).reshape(n, wide, 256)
+        start(3 + part, blocks(mixed, part), planes.at[part])
+        planes[part, me] = mixed[part, me]
+
+    image_columns(0, 0, 96, 0)
+    image_columns(160, 32, 128, 128)
+    send_columns(
+        0,
+        jnp.concatenate(
+            [exact_dot(blur_first, acid[:96]), exact_dot(blur_last, acid[160:])], axis=0
+        ),
+    )
+    image_columns(96, 32, 96, 64)
+    send_columns(1, exact_dot(blur_middle, acid[48:208]))
+    intensity_ref[...] = image[...].T
+    mix_planes(0)
+    mix_planes(1)
     sent(0, point_source, points)
-    sent(1, column_source, columns)
-    receive(2, plane_source, planes, block_of)
-    latent_ref[...] = planes[...].reshape(256, 256).T
-    sent(2, plane_source, planes, block_of)
+    receive(3, blocks(mixed, 0), planes.at[0])
+    outer = planes[0].reshape(size, 256)
+    latent_ref[:, :64] = outer[:64].T
+    latent_ref[:, 192:] = outer[64:].T
+    receive(4, blocks(mixed, 1), planes.at[1])
+    latent_ref[:, 64:192] = planes[1].reshape(size, 256).T
+    for part in range(2):
+        sent(1 + part, blocks(along, part), columns.at[part])
+        sent(3 + part, blocks(mixed, part), planes.at[part])
 
 
 def plane_per_device(
     layout_mask, source_coords, source_weights, focus_steps, pupil_taps, blur_x, blur_y, blur_z
 ):
     n = lax.axis_size("src")
-    wide = layout_mask.shape[1] // n
+    wide = layout_mask.shape[1] // n // 2
     square = jax.ShapeDtypeStruct((256, 256), jnp.float32)
     full = pltpu.VMEM((256, 256), jnp.float32)
-    parts = pltpu.VMEM((n, wide, 256), jnp.float32)
+    parts = pltpu.VMEM((2, n, wide, 256), jnp.float32)
     vmem = pl.BlockSpec(memory_space=pltpu.VMEM)
     hbm = pl.BlockSpec(memory_space=pltpu.HBM)
     arguments = (
@@ -408,12 +469,13 @@
         + [pltpu.SemaphoreType.DMA((8,)), pltpu.VMEM((8, lanes), jnp.float32)]
         + [pltpu.VMEM((24, 128), jnp.float32)] * 4
         + [
-            pltpu.VMEM((4, 512, 256), jnp.bfloat16),
+            pltpu.VMEM((4, 256, 512), jnp.bfloat16),
             pltpu.VMEM((shifts, 256, 512), jnp.bfloat16),
-            pltpu.VMEM((shifts, 512, 512), jnp.bfloat16),
+            pltpu.VMEM((shifts, 256, 256), jnp.bfloat16),
             full,
             full,
             full,
+            pltpu.VMEM((n * wide, n * wide), jnp.float32),
             pltpu.VMEM((1, 128), jnp.int32),
             pltpu.VMEM((n, 1, 128), jnp.int32),
             pltpu.SMEM((n, 1, 128), jnp.int32),
@@ -421,8 +483,8 @@
             parts,
             parts,
             parts,
-            pltpu.SemaphoreType.DMA((3, n)),
-            pltpu.SemaphoreType.DMA((3, n)),
+            pltpu.SemaphoreType.DMA((5, n)),
+            pltpu.SemaphoreType.DMA((5, n)),
             pltpu.SemaphoreType.DMA,
         ],
         compiler_params=pltpu.CompilerParams(

time: 34.5 us -> 31.6 us (0.916)
  Pallas kernels: 31.3 us -> 28.3 us
    pallas_call x1, Pallas kernels: 31.3 us -> 28.3 us  [plane_per_device(): pl.pallas_call(lambda *refs: plane_kernel(n, wide, *refs), out_shape=(squ...]
where the time goes in v1:
time: 31.6 us; the launch traced here: 31.4 us
  Pallas kernels  28.3 us (90%)
  local copies, waits for them, and re-layouts  2.42 us (8%)
  between operations  0.65 us (2%)
    pallas_call x1, Pallas kernels, plane_per_device(): pl.pallas_call(lambda *refs: plane_kernel(n, wide, *refs), out_shape=(squ...  28.3 us
    unnamed x4, local copies, waits for them, and re-layouts  2.42 us

profile of v1, /device:TPU:0, one launch (start us, length us, event | category | flops | bytes accessed | tf_op | source)
XLA Modules:
  0.0 31.4 jit_solution(4070276611995564296)
XLA Ops:
  0.6 28.3 %shard_map.95 = (f32[256,256]{1,0:T(8,128)}, f32[256,256]{1,0:T(8,128)}) custom-call(s32[256,256]{1,0:T(8,128)} %refs_0_.1, s32[2,2]{1,0:T(2,128)} %refs_1_.1, s32[2]{0:T(128)} %refs_2_.1, s32[16]{0:T(128)} %refs_3_.1, f32[48]{0:T(128)} %refs_4_.1, f32[31]{0:T(128)} %refs_5_.1, f32[31]{0:T(128)} %refs_6_.1, f32[31]{0:T(128)} %refs_7_.1), custom_call_target="tpu_custom_call" | custom-call | tf_op jit(solution)/shard_map/pallas_call | solution.py:462
  29.0 0.0 copy-start
  29.0 1.7 %copy.12 = f32[256,256]{1,0:T(8,128)} copy(f32[256,256]{1,0:T(8,128)} %get-tuple-element.4) | data formatting | bytes 524288
  30.7 0.0 copy-done
  30.7 0.7 %copy.13 = f32[256,256]{1,0:T(8,128)} copy(f32[256,256]{1,0:T(8,128)S(1)} %copy-done) | data formatting | bytes 524288
Async XLA Ops:
  29.0 1.7 %copy-start = (f32[256,256]{1,0:T(8,128)S(1)}, f32[256,256]{1,0:T(8,128)}, u32[]{:S(2)}) copy-start(f32[256,256]{1,0:T(8,128)} %get-tuple-element.5) | copy-start | bytes 786436

commit v2 on v1

--- a/solution.py
+++ b/solution.py
@@ -446,6 +446,17 @@
         sent(3 + part, blocks(mixed, part), planes.at[part])
 
 
+def store_kernel(intensity_ref, latent_ref, intensity_hbm, latent_hbm, sems):
+    stores = [
+        pltpu.make_async_copy(intensity_ref, intensity_hbm, sems.at[0]),
+        pltpu.make_async_copy(latent_ref, latent_hbm, sems.at[1]),
+    ]
+    for store in stores:
+        store.start()
+    for store in stores:
+        store.wait()
+
+
 def plane_per_device(
     layout_mask, source_coords, source_weights, focus_steps, pupil_taps, blur_x, blur_y, blur_z
 ):
@@ -459,7 +470,7 @@
     arguments = (
         source_coords, source_weights, focus_steps, pupil_taps, blur_x, blur_y, blur_z
     )
-    return pl.pallas_call(
+    made = pl.pallas_call(
         lambda *refs: plane_kernel(n, wide, *refs),
         out_shape=(square, square),
         in_specs=[hbm] * 8,
@@ -488,9 +499,16 @@
             pltpu.SemaphoreType.DMA,
         ],
         compiler_params=pltpu.CompilerParams(
-            vmem_limit_bytes=64 * 2**20 - 2**17, collective_id=0, has_side_effects=True
+            vmem_limit_bytes=32 * 2**20, collective_id=0, has_side_effects=True
         ),
-    )(layout_mask, *arguments)
+    )(*[pltpu.with_memory_space_constraint(value, pltpu.HBM) for value in (layout_mask, *arguments)])
+    return pl.pallas_call(
+        store_kernel,
+        out_shape=(square, square),
+        in_specs=[vmem] * 2,
+        out_specs=(hbm, hbm),
+        scratch_shapes=[pltpu.SemaphoreType.DMA((2,))],
+    )(*[pltpu.with_memory_space_constraint(value, pltpu.VMEM) for value in made])
 
 
 def solution(mesh):

time: 31.6 us -> 29.1 us (0.921)
  local copies, waits for them, and re-layouts: 2.42 us -> 0 us
    unnamed x4 -> x0, local copies, waits for them, and re-layouts: 2.42 us -> none
    pallas_call x0 -> x1, Pallas kernels: none -> 0.81 us  [plane_per_device(): pl.pallas_call(store_kernel, out_shape=(square, square), in_specs=[vmem]...]
    pallas_call x1, Pallas kernels: 28.3 us -> 27.5 us  [plane_per_device(): pl.pallas_call(lambda *refs: plane_kernel(n, wide, *refs), out_shape=(squ...]
where the time goes in v2:
time: 29.1 us; the launch traced here: 29 us
  Pallas kernels  28.4 us (98%)
  between operations  0.64 us (2%)
    pallas_call x1, Pallas kernels, plane_per_device(): pl.pallas_call(lambda *refs: plane_kernel(n, wide, *refs), out_shape=(squ...  27.5 us
    pallas_call x1, Pallas kernels, plane_per_device(): pl.pallas_call(store_kernel, out_shape=(square, square), in_specs=[vmem]...  0.81 us

profile of v2, /device:TPU:0, one launch (start us, length us, event | category | flops | bytes accessed | tf_op | source)
XLA Modules:
  0.0 29.0 jit_solution(527970918851304774)
XLA Ops:
  0.6 27.5 %shard_map.95 = (f32[256,256]{1,0:T(8,128)S(1)}, f32[256,256]{1,0:T(8,128)S(1)}) custom-call(s32[256,256]{1,0:T(8,128)} %refs_0_.1, s32[2,2]{1,0:T(2,128)} %refs_1_.1, s32[2]{0:T(128)} %refs_2_.1, s32[16]{0:T(128)} %refs_3_.1, f32[48]{0:T(128)} %refs_4_.1, f32[31]{0:T(128)} %refs_5_.1, f32[31]{0:T(128)} %refs_6_.1, f32[31]{0:T(128)} %refs_7_.1), custom_call_target="tpu_custom_call" | custom-call | tf_op jit(solution)/shard_map/pallas_call | solution.py:473
  28.2 0.8 %shard_map.96 = (f32[256,256]{1,0:T(8,128)}, f32[256,256]{1,0:T(8,128)}) custom-call(f32[256,256]{1,0:T(8,128)S(1)} %get-tuple-element.4.intensity_ref, f32[256,256]{1,0:T(8,128)S(1)} %get-tuple-element.5.latent_ref), custom_call_target="tpu_custom_call" | custom-call | tf_op jit(solution)/shard_map/pallas_call | solution.py:505

commit v3 on v2

--- a/solution.py
+++ b/solution.py
@@ -173,70 +173,52 @@
     imag_ref[...] = amplitude * jnp.sin(phase)
 
 
-def toeplitz_tiles(row, position, blocks):
+def toeplitz_tiles(row, position, blocks, dtype=jnp.float32):
     base = pltpu.roll(jnp.broadcast_to(row, (16, 128)), 0, 1, stride=1, stride_axis=0)
     apart = lax.broadcasted_iota(jnp.int32, (16, 128), 1) - lax.broadcasted_iota(
         jnp.int32, (16, 128), 0
     )
+    base = base.astype(dtype)
     tiles = {}
     for block in blocks:
         turn = 16 * block - position
         tile = pltpu.roll(base, turn % 128, 1) if turn % 128 else base
         if 127 - turn >= 128:
-            tile = jnp.where(apart < 128 + turn, tile, 0.0)
+            tile = jnp.where(apart < 128 + turn, tile, jnp.zeros_like(tile))
         if -15 - turn < -80:
-            tile = jnp.where(apart >= turn - 80, tile, 0.0)
+            tile = jnp.where(apart >= turn - 80, tile, jnp.zeros_like(tile))
         tiles[block] = tile
     return tiles
 
 
-def build_columns(forward_real, forward_imag, shapes):
-    def one_shift(shift):
-        row = pl.ds(shift, 1)
-        real = toeplitz_tiles(forward_real[row, :], 24, range(8))
-        imag = toeplitz_tiles(forward_imag[row, :], 24, range(8))
-        for j in range(8):
-            re, im = real[j].astype(jnp.bfloat16), imag[j].astype(jnp.bfloat16)
-            upper, lower = slice(16 * j, 16 * j + 16), slice(128 + 16 * j, 144 + 16 * j)
-            shapes[shift, upper, :128] = re
-            shapes[shift, upper, 128:] = -im
-            shapes[shift, lower, :128] = im
-            shapes[shift, lower, 128:] = re
-
-    def four_shifts(step, carry):
-        for place in range(4):
-            one_shift(4 * step + place)
-        return carry
-
-    lax.fori_loop(0, shifts // 4, four_shifts, 0)
-    one_shift(shifts - 1)
-
-
-def build_fields(back_real, back_imag, mask_ref, slots, fields):
+def build_tables(forward_real, forward_imag, back_real, back_imag, mask_ref, slots, shapes, fields):
     mask_turned = mask_ref[...].astype(jnp.float32).T.astype(jnp.bfloat16)
 
     def one_shift(shift, slot):
         row = pl.ds(shift, 1)
+        real = toeplitz_tiles(forward_real[row, :], 24, range(8), jnp.bfloat16)
+        imag = toeplitz_tiles(forward_imag[row, :], 24, range(8), jnp.bfloat16)
+        for j in range(8):
+            upper, lower = slice(16 * j, 16 * j + 16), slice(128 + 16 * j, 144 + 16 * j)
+            shapes[shift, upper, :128] = real[j]
+            shapes[shift, upper, 128:] = -imag[j]
+            shapes[shift, lower, :128] = imag[j]
+            shapes[shift, lower, 128:] = real[j]
         for side, source in ((0, back_real), (256, back_imag)):
-            tiles = toeplitz_tiles(source[row, :], 23, range(-2, 10))
+            tiles = toeplitz_tiles(source[row, :], 23, range(-2, 10), jnp.bfloat16)
             for block, tile in tiles.items():
-                value = tile.astype(jnp.bfloat16)
                 if block >= 0:
-                    slots[slot, 16 * block : 16 * block + 16, side : side + 128] = value
+                    slots[slot, 16 * block : 16 * block + 16, side : side + 128] = tile
                 if block < 8:
                     top = 16 * block + 128
-                    slots[slot, top : top + 16, side + 128 : side + 256] = value
-        fields[shift] = jnp.dot(
-            mask_turned, slots[slot], preferred_element_type=jnp.float32
-        ).astype(jnp.bfloat16)
-
-    def four_shifts(step, carry):
-        for slot in range(4):
-            one_shift(4 * step + slot, slot)
-        return carry
-
-    lax.fori_loop(0, shifts // 4, four_shifts, 0)
-    one_shift(shifts - 1, 0)
+                    slots[slot, top : top + 16, side + 128 : side + 256] = tile
+        for side in (0, 256):
+            fields[shift, :, side : side + 256] = jnp.dot(
+                mask_turned, slots[slot, :, side : side + 256], preferred_element_type=jnp.float32
+            ).astype(jnp.bfloat16)
+
+    for shift in range(shifts):
+        one_shift(shift, shift % 4)
 
 
 def lane_row(count, value):
@@ -275,8 +257,8 @@
         return pltpu.make_async_remote_copy(
             src_ref=source(off),
             dst_ref=target.at[slot],
-            send_sem=send_sems.at[phase, off],
-            recv_sem=recv_sems.at[phase, off],
+            send_sem=send_sems.at[phase],
+            recv_sem=recv_sems.at[phase],
             device_id=peer(off),
             device_id_type=pl.DeviceIdType.MESH,
         )
@@ -284,13 +266,22 @@
     def start(phase, source, target):
         each(lambda off: copy(phase, source, target, off, me).start())
 
-    def receive(phase, source, target):
-        each(
-            lambda off: copy(phase, source, target, off, lax.rem(me + n - off, n)).wait_recv()
-        )
-
-    def sent(phase, source, target):
-        each(lambda off: copy(phase, source, target, off, me).wait_send())
+    def whole(phase, target):
+        others = target.at[pl.ds(0, n - 1)]
+        return pltpu.make_async_remote_copy(
+            src_ref=others,
+            dst_ref=others,
+            send_sem=send_sems.at[phase],
+            recv_sem=recv_sems.at[phase],
+            device_id=peer(1),
+            device_id_type=pl.DeviceIdType.MESH,
+        )
+
+    def receive(phase, target):
+        whole(phase, target).wait_recv()
+
+    def sent(phase, target):
+        whole(phase, target).wait_send()
 
     def blocks(ref, part):
         return lambda off: ref.at[part, lax.rem(me + off, n)]
@@ -331,11 +322,10 @@
     focus = focus_ref[me].astype(jnp.float32)
     store_taps(rows, 0, focus, 1.0, t0, t1, tap_count)
     store_taps(rows, 1, focus, -1.0, t2, t3, tap_count)
-    build_columns(t0, t1, shapes)
     pl.semaphore_wait(barrier, n - 1)
     point_source = lambda off: own
-    start(0, point_source, points)
-    build_fields(t2, t3, mask_ref, slots, fields)
+    each(lambda off: copy(0, point_source, points, n - off, me).start())
+    build_tables(t0, t1, t2, t3, mask_ref, slots, shapes, fields)
     image[...] = jnp.zeros_like(image)
     tiles = toeplitz_tiles(rows[2:3, :128], 15, range(-1, 9))
     blank = jnp.zeros((96, 128), jnp.float32)
@@ -362,7 +352,7 @@
     for lag in range(1 - n, n):
         mixing = jnp.where(distance == lag * wide, blur_z_ref[lag + n - 1] / n, mixing)
     mix[...] = mixing
-    receive(0, point_source, points)
+    receive(0, points)
     to_smem = pltpu.make_async_copy(points, points_smem, local_sem)
     to_smem.start()
     to_smem.wait()
@@ -403,7 +393,7 @@
         columns[part, me] = along[part, me]
 
     def mix_planes(part):
-        receive(1 + part, blocks(along, part), columns.at[part])
+        receive(1 + part, columns.at[part])
         stack = columns[part].reshape(size, 256)
         zero = jnp.zeros((wide, 128), jnp.float32)
         along_y = (
@@ -434,16 +424,17 @@
     intensity_ref[...] = image[...].T
     mix_planes(0)
     mix_planes(1)
-    sent(0, point_source, points)
-    receive(3, blocks(mixed, 0), planes.at[0])
+    sent(0, points)
+    sent(1, columns.at[0])
+    sent(2, columns.at[1])
+    sent(3, planes.at[0])
+    receive(3, planes.at[0])
     outer = planes[0].reshape(size, 256)
     latent_ref[:, :64] = outer[:64].T
     latent_ref[:, 192:] = outer[64:].T
-    receive(4, blocks(mixed, 1), planes.at[1])
+    sent(4, planes.at[1])
+    receive(4, planes.at[1])
     latent_ref[:, 64:192] = planes[1].reshape(size, 256).T
-    for part in range(2):
-        sent(1 + part, blocks(along, part), columns.at[part])
-        sent(3 + part, blocks(mixed, part), planes.at[part])
 
 
 def store_kernel(intensity_ref, latent_ref, intensity_hbm, latent_hbm, sems):
@@ -494,8 +485,8 @@
             parts,
             parts,
             parts,
-            pltpu.SemaphoreType.DMA((5, n)),
-            pltpu.SemaphoreType.DMA((5, n)),
+            pltpu.SemaphoreType.DMA((5,)),
+            pltpu.SemaphoreType.DMA((5,)),
             pltpu.SemaphoreType.DMA,
         ],
         compiler_params=pltpu.CompilerParams(

time: 29.1 us -> 27 us (0.928)
  Pallas kernels: 28.4 us -> 26.3 us
    pallas_call x1, Pallas kernels: 27.5 us -> 25.4 us  [plane_per_device(): pl.pallas_call(lambda *refs: plane_kernel(n, wide, *refs), out_shape=(squ...]
where the time goes in v3:
time: 27 us; the launch traced here: 26.9 us
  Pallas kernels  26.3 us (97%)
  between operations  0.64 us (2%)
    pallas_call x1, Pallas kernels, plane_per_device(): pl.pallas_call(lambda *refs: plane_kernel(n, wide, *refs), out_shape=(squ...  25.4 us
    pallas_call x1, Pallas kernels, plane_per_device(): pl.pallas_call(store_kernel, out_shape=(square, square), in_specs=[vmem]...  0.81 us

profile of v3, /device:TPU:0, one launch (start us, length us, event | category | flops | bytes accessed | tf_op | source)
XLA Modules:
  0.0 26.9 jit_solution(3300855935210588789)
XLA Ops:
  0.6 25.4 %shard_map.95 = (f32[256,256]{1,0:T(8,128)S(1)}, f32[256,256]{1,0:T(8,128)S(1)}) custom-call(s32[256,256]{1,0:T(8,128)} %refs_0_.1, s32[2,2]{1,0:T(2,128)} %refs_1_.1, s32[2]{0:T(128)} %refs_2_.1, s32[16]{0:T(128)} %refs_3_.1, f32[48]{0:T(128)} %refs_4_.1, f32[31]{0:T(128)} %refs_5_.1, f32[31]{0:T(128)} %refs_6_.1, f32[31]{0:T(128)} %refs_7_.1), custom_call_target="tpu_custom_call" | custom-call | tf_op jit(solution)/shard_map/pallas_call | solution.py:464
  26.1 0.8 %shard_map.96 = (f32[256,256]{1,0:T(8,128)}, f32[256,256]{1,0:T(8,128)}) custom-call(f32[256,256]{1,0:T(8,128)S(1)} %get-tuple-element.4.intensity_ref, f32[256,256]{1,0:T(8,128)S(1)} %get-tuple-element.5.latent_ref), custom_call_target="tpu_custom_call" | custom-call | tf_op jit(solution)/shard_map/pallas_call | solution.py:496

commit v4 on v3

--- a/solution.py
+++ b/solution.py
@@ -304,8 +304,7 @@
     for fetch in fetches:
         fetch.start()
     each(signal)
-    slots[...] = jnp.zeros_like(slots)
-    for fetch in fetches:
+    for fetch in fetches[:2]:
         fetch.wait()
     lane = lax.broadcasted_iota(jnp.int32, (1, 128), 1)
     packed = jnp.zeros((1, 128), jnp.int32)
@@ -315,6 +314,17 @@
         packed = jnp.where(lane == 3 * s + 2, weights_ref[s], packed)
     own[...] = packed
     points[me] = packed
+    point_source = lambda off: own
+
+    def send_point():
+        pl.semaphore_wait(barrier, n - 1)
+        each(lambda off: copy(0, point_source, points, n - off, me).start())
+
+    late = me >= n // 2
+    pl.when(late)(send_point)
+    slots[...] = jnp.zeros_like(slots)
+    for fetch in fetches[2:]:
+        fetch.wait()
     rows[0:1, :] = lane_row(tap_count, lambda t: taps_ref[t])
     rows[1:2, :] = lane_row(tap_count, lambda t: taps_ref[tap_count - 1 - t])
     rows[2:3, :] = lane_row(blur_count, lambda t: blur_x_ref[t] / blur_count)
@@ -322,19 +332,22 @@
     focus = focus_ref[me].astype(jnp.float32)
     store_taps(rows, 0, focus, 1.0, t0, t1, tap_count)
     store_taps(rows, 1, focus, -1.0, t2, t3, tap_count)
-    pl.semaphore_wait(barrier, n - 1)
-    point_source = lambda off: own
-    each(lambda off: copy(0, point_source, points, n - off, me).start())
+    pl.when(jnp.logical_not(late))(send_point)
     build_tables(t0, t1, t2, t3, mask_ref, slots, shapes, fields)
     image[...] = jnp.zeros_like(image)
     tiles = toeplitz_tiles(rows[2:3, :128], 15, range(-1, 9))
-    blank = jnp.zeros((96, 128), jnp.float32)
-    blur_first = jnp.concatenate([tiles[j] for j in range(4)], axis=0)[:, :96]
-    blur_last = jnp.concatenate([tiles[j] for j in range(2, 6)], axis=0)[:, :96]
-    blur_middle = jnp.concatenate(
+    blank = jnp.zeros((112, 128), jnp.float32)
+    blur_low = jnp.concatenate(
+        [
+            jnp.concatenate([tiles[j] for j in range(8)], axis=0),
+            jnp.concatenate([blank, tiles[-1]], axis=0)[:, :16],
+        ],
+        axis=1,
+    )
+    blur_high = jnp.concatenate(
         [
             jnp.concatenate([tiles[j] for j in range(1, 9)], axis=0),
-            jnp.concatenate([blank, tiles[-1], tiles[0]], axis=0)[:, :32],
+            jnp.concatenate([blank[:96], tiles[-1], tiles[0]], axis=0)[:, :16],
         ],
         axis=1,
     )
@@ -412,15 +425,10 @@
         planes[part, me] = mixed[part, me]
 
     image_columns(0, 0, 96, 0)
+    image_columns(96, 32, 96, 64)
+    send_columns(0, exact_dot(blur_low, acid[:144]))
     image_columns(160, 32, 128, 128)
-    send_columns(
-        0,
-        jnp.concatenate(
-            [exact_dot(blur_first, acid[:96]), exact_dot(blur_last, acid[160:])], axis=0
-        ),
-    )
-    image_columns(96, 32, 96, 64)
-    send_columns(1, exact_dot(blur_middle, acid[48:208]))
+    send_columns(1, exact_dot(blur_high, acid[112:]))
     intensity_ref[...] = image[...].T
     mix_planes(0)
     mix_planes(1)
@@ -429,12 +437,10 @@
     sent(2, columns.at[1])
     sent(3, planes.at[0])
     receive(3, planes.at[0])
-    outer = planes[0].reshape(size, 256)
-    latent_ref[:, :64] = outer[:64].T
-    latent_ref[:, 192:] = outer[64:].T
+    latent_ref[:, :size] = planes[0].reshape(size, 256).T
     sent(4, planes.at[1])
     receive(4, planes.at[1])
-    latent_ref[:, 64:192] = planes[1].reshape(size, 256).T
+    latent_ref[:, size:] = planes[1].reshape(size, 256).T
 
 
 def store_kernel(intensity_ref, latent_ref, intensity_hbm, latent_hbm, sems):

time: 27 us -> 26.7 us (0.989)
  Pallas kernels: 26.3 us -> 25.9 us
    pallas_call x1, Pallas kernels: 25.4 us -> 25.1 us  [plane_per_device(): pl.pallas_call(lambda *refs: plane_kernel(n, wide, *refs), out_shape=(squ...]
where the time goes in v4:
time: 26.7 us; the launch traced here: 26.6 us
  Pallas kernels  25.9 us (97%)
  between operations  0.64 us (2%)
    pallas_call x1, Pallas kernels, plane_per_device(): pl.pallas_call(lambda *refs: plane_kernel(n, wide, *refs), out_shape=(squ...  25.1 us
    pallas_call x1, Pallas kernels, plane_per_device(): pl.pallas_call(store_kernel, out_shape=(square, square), in_specs=[vmem]...  0.81 us

profile of v4, /device:TPU:0, one launch (start us, length us, event | category | flops | bytes accessed | tf_op | source)
XLA Modules:
  0.0 26.6 jit_solution(2650036681031601077)
XLA Ops:
  0.6 25.1 %shard_map.95 = (f32[256,256]{1,0:T(8,128)S(1)}, f32[256,256]{1,0:T(8,128)S(1)}) custom-call(s32[256,256]{1,0:T(8,128)} %refs_0_.1, s32[2,2]{1,0:T(2,128)} %refs_1_.1, s32[2]{0:T(128)} %refs_2_.1, s32[16]{0:T(128)} %refs_3_.1, f32[48]{0:T(128)} %refs_4_.1, f32[31]{0:T(128)} %refs_5_.1, f32[31]{0:T(128)} %refs_6_.1, f32[31]{0:T(128)} %refs_7_.1), custom_call_target="tpu_custom_call" | custom-call | tf_op jit(solution)/shard_map/pallas_call | solution.py:470
  25.8 0.8 %shard_map.96 = (f32[256,256]{1,0:T(8,128)}, f32[256,256]{1,0:T(8,128)}) custom-call(f32[256,256]{1,0:T(8,128)S(1)} %get-tuple-element.4.intensity_ref, f32[256,256]{1,0:T(8,128)S(1)} %get-tuple-element.5.latent_ref), custom_call_target="tpu_custom_call" | custom-call | tf_op jit(solution)/shard_map/pallas_call | solution.py:502

commit v5 on v4

--- a/solution.py
+++ b/solution.py
@@ -123,16 +123,17 @@
 devices_unrolled = 16
 
 
+def halves(value):
+    high = value.astype(jnp.bfloat16)
+    return high, (value - high.astype(jnp.float32)).astype(jnp.bfloat16)
+
+
 def exact_dot(left, right):
-    def halves(value):
-        high = value.astype(jnp.bfloat16)
-        return high, (value - high.astype(jnp.float32)).astype(jnp.bfloat16)
-
     def product(a, b):
         return jnp.dot(a, b, preferred_element_type=jnp.float32)
 
-    left_high, left_low = halves(left)
-    right_high, right_low = halves(right)
+    left_high, left_low = left if isinstance(left, tuple) else halves(left)
+    right_high, right_low = right if isinstance(right, tuple) else halves(right)
     return (
         product(left_high, right_low) + product(left_low, right_high)
     ) + product(left_high, right_high)
@@ -233,8 +234,7 @@
     n, wide, mask_hbm, coords_hbm, weights_hbm, focus_hbm, taps_hbm, blur_x_hbm, blur_y_hbm,
     blur_z_hbm, intensity_ref, latent_ref, mask_ref, coords_ref, weights_ref, focus_ref, taps_ref,
     blur_x_ref, blur_y_ref, blur_z_ref, arg_sems, rows, t0, t1, t2, t3, slots, fields, shapes, image,
-    acid, centre, mix, own, points, points_smem, along, columns, mixed, planes, send_sems, recv_sems,
-    local_sem,
+    acid, centre, centre_parts, edge_parts, mix_parts, own, points, points_smem, along, columns, mixed, planes, send_sems, recv_sems,
 ):
     me = lax.axis_index("src")
     group = lax.axis_index("groups")
@@ -364,11 +364,17 @@
     mixing = jnp.zeros((size, size), jnp.float32)
     for lag in range(1 - n, n):
         mixing = jnp.where(distance == lag * wide, blur_z_ref[lag + n - 1] / n, mixing)
-    mix[...] = mixing
+    for ref, value in (
+        (centre_parts, centre[...]),
+        (edge_parts, jnp.concatenate([after, pad, pad, before], axis=0)),
+        (mix_parts, mixing),
+    ):
+        ref[0], ref[1] = halves(value)
     receive(0, points)
-    to_smem = pltpu.make_async_copy(points, points_smem, local_sem)
-    to_smem.start()
-    to_smem.wait()
+    for device in range(n):
+        row = points[device]
+        for item in range(3 * local):
+            points_smem[device, 0, item] = row[0, item]
 
     def image_columns(left, low, high, first):
         count = high - low
@@ -409,18 +415,17 @@
         receive(1 + part, columns.at[part])
         stack = columns[part].reshape(size, 256)
         zero = jnp.zeros((wide, 128), jnp.float32)
-        along_y = (
-            exact_dot(stack, centre[...])
-            + exact_dot(
-                jnp.concatenate([zero, stack[:-wide, 128:]], axis=0),
-                jnp.concatenate([pad, before], axis=0),
-            )
-            + exact_dot(
-                jnp.concatenate([stack[wide:, :128], zero], axis=0),
-                jnp.concatenate([after, pad], axis=0),
-            )
-        )
-        mixed[part] = exact_dot(mix[...], along_y).reshape(n, wide, 256)
+        along_y = exact_dot(stack, (centre_parts[0], centre_parts[1])) + exact_dot(
+            jnp.concatenate(
+                [
+                    jnp.concatenate([stack[wide:, :128], zero], axis=0),
+                    jnp.concatenate([zero, stack[:-wide, 128:]], axis=0),
+                ],
+                axis=1,
+            ),
+            (edge_parts[0], edge_parts[1]),
+        )
+        mixed[part] = exact_dot((mix_parts[0], mix_parts[1]), along_y).reshape(n, wide, 256)
         start(3 + part, blocks(mixed, part), planes.at[part])
         planes[part, me] = mixed[part, me]
 
@@ -429,9 +434,9 @@
     send_columns(0, exact_dot(blur_low, acid[:144]))
     image_columns(160, 32, 128, 128)
     send_columns(1, exact_dot(blur_high, acid[112:]))
-    intensity_ref[...] = image[...].T
     mix_planes(0)
     mix_planes(1)
+    intensity_ref[...] = image[...].T
     sent(0, points)
     sent(1, columns.at[0])
     sent(2, columns.at[1])
@@ -483,7 +488,9 @@
             full,
             full,
             full,
-            pltpu.VMEM((n * wide, n * wide), jnp.float32),
+            pltpu.VMEM((2, 256, 256), jnp.bfloat16),
+            pltpu.VMEM((2, 256, 256), jnp.bfloat16),
+            pltpu.VMEM((2, n * wide, n * wide), jnp.bfloat16),
             pltpu.VMEM((1, 128), jnp.int32),
             pltpu.VMEM((n, 1, 128), jnp.int32),
             pltpu.SMEM((n, 1, 128), jnp.int32),
@@ -493,7 +500,6 @@
             parts,
             pltpu.SemaphoreType.DMA((5,)),
             pltpu.SemaphoreType.DMA((5,)),
-            pltpu.SemaphoreType.DMA,
         ],
         compiler_params=pltpu.CompilerParams(
             vmem_limit_bytes=32 * 2**20, collective_id=0, has_side_effects=True

time: 26.7 us -> 26.2 us (0.981)
  Pallas kernels: 25.9 us -> 25.4 us
    pallas_call x1, Pallas kernels: 25.1 us -> 24.6 us  [plane_per_device(): pl.pallas_call(lambda *refs: plane_kernel(n, wide, *refs), out_shape=(squ...]
where the time goes in v5:
time: 26.2 us; the launch traced here: 26 us
  Pallas kernels  25.4 us (97%)
  between operations  0.64 us (2%)
    pallas_call x1, Pallas kernels, plane_per_device(): pl.pallas_call(lambda *refs: plane_kernel(n, wide, *refs), out_shape=(squ...  24.6 us
    pallas_call x1, Pallas kernels, plane_per_device(): pl.pallas_call(store_kernel, out_shape=(square, square), in_specs=[vmem]...  0.81 us

profile of v5, /device:TPU:0, one launch (start us, length us, event | category | flops | bytes accessed | tf_op | source)
XLA Modules:
  0.0 26.0 jit_solution(11618603576514102208)
XLA Ops:
  0.6 24.6 %shard_map.95 = (f32[256,256]{1,0:T(8,128)S(1)}, f32[256,256]{1,0:T(8,128)S(1)}) custom-call(s32[256,256]{1,0:T(8,128)} %refs_0_.1, s32[2,2]{1,0:T(2,128)} %refs_1_.1, s32[2]{0:T(128)} %refs_2_.1, s32[16]{0:T(128)} %refs_3_.1, f32[48]{0:T(128)} %refs_4_.1, f32[31]{0:T(128)} %refs_5_.1, f32[31]{0:T(128)} %refs_6_.1, f32[31]{0:T(128)} %refs_7_.1), custom_call_target="tpu_custom_call" | custom-call | tf_op jit(solution)/shard_map/pallas_call | solution.py:475
  25.2 0.8 %shard_map.96 = (f32[256,256]{1,0:T(8,128)}, f32[256,256]{1,0:T(8,128)}) custom-call(f32[256,256]{1,0:T(8,128)S(1)} %get-tuple-element.4.intensity_ref, f32[256,256]{1,0:T(8,128)S(1)} %get-tuple-element.5.latent_ref), custom_call_target="tpu_custom_call" | custom-call | tf_op jit(solution)/shard_map/pallas_call | solution.py:508
